TPU v7x, 32 devices: a whole 2x2x4 slice. The times are simulated.
32 devices in a mesh: section: 4 (over z), tm: 4 (over y, x), batch: 2 (over core).
Axes of the slice: x: 2, y: 2, z: 4, core: 2. Of those that a mesh axis runs over, the one named last changes fastest.
Arguments:
- acts: bfloat16 [4, 4, 8, 6, 10240], P('section', 'batch', 'tm'), may hold values from -6 to 6
- cot: bfloat16 [4, 8, 6, 10240], P('batch', 'tm'), may hold values from -6 to 6
- spatial_weight: bfloat16 [4, 9, 64, 64], P('section'), may hold values from -0.25 to 0.25
- temporal_weight: bfloat16 [4, 3, 64, 64], P('section'), may hold values from -0.4375 to 0.4375
Outputs:
- grad_in: bfloat16 [4, 4, 8, 6, 10240], P('section', 'batch', 'tm')
- grad_spatial: float32 [4, 9, 64, 64], P('section')
- grad_temporal: float32 [4, 3, 64, 64], P('section')
All inputs are finite; a program needn't handle non-finite values.
Results may differ from a plain program's by a relative error of at most 0.012.
Values may be sent and summed in bfloat16 or wider, within the bound.
A program may use at most 128 MiB of HBM per device.

v0:
```python
import jax
import jax.numpy as jnp
from jax import lax
from jax.sharding import PartitionSpec as P

TIME_DILATION = 2


def from_behind(value, axis, steps):
    count = lax.axis_size(axis)
    first, last = (max(0, -steps), min(count, count - steps))
    return lax.ppermute(value, axis, [(source, source + steps) for source in range(first, last)])


def split_pixels(a, chans):
    return a.reshape(a.shape[:-1] + (a.shape[-1] // chans, chans))


def paired_kernel(kernel):
    return jnp.kron(jnp.eye(2, dtype=kernel.dtype), kernel)


def spatial_fwd(x, ws):
    rows, width = (x.shape[1], x.shape[2])
    chans = ws.shape[-1]
    padded = jnp.pad(x, ((0, 0), (1, 1), (chans, chans)))
    total = jnp.zeros(x.shape, jnp.float32)
    for i in range(3):
        for j in range(3):
            piece = split_pixels(padded[:, i : i + rows, j * chans : j * chans + width], 2 * chans)
            total = total + jnp.einsum(
                "nrpa,ab->nrpb",
                piece,
                paired_kernel(ws[3 * i + j]),
                preferred_element_type=jnp.float32,
            ).reshape(x.shape)
    return total


def spatial_back(gz, x, ws):
    rows, width = (x.shape[1], x.shape[2])
    chans = ws.shape[-1]
    xpad = jnp.pad(x, ((0, 0), (1, 1), (chans, chans)))
    gradient_padded = jnp.pad(gz, ((0, 0), (1, 1), (chans, chans)))
    gz_pairs = split_pixels(gz, 2 * chans)
    total = jnp.zeros(x.shape, jnp.float32)
    grads = []
    for i in range(3):
        for j in range(3):
            gpiece = split_pixels(
                gradient_padded[:, 2 - i : 2 - i + rows, (2 - j) * chans : (2 - j) * chans + width],
                2 * chans,
            )
            total = total + jnp.einsum(
                "nrpb,ab->nrpa",
                gpiece,
                paired_kernel(ws[3 * i + j]),
                preferred_element_type=jnp.float32,
            ).reshape(x.shape)
            xpiece = split_pixels(xpad[:, i : i + rows, j * chans : j * chans + width], 2 * chans)
            square = jnp.einsum(
                "nrpa,nrpb->ab", xpiece, gz_pairs, preferred_element_type=jnp.float32
            )
            grads.append(square[:chans, :chans] + square[chans:, chans:])
    return (total, jnp.stack(grads))


def temporal_back(h, gradient_piece, gradient_padded, dilation_step, wt):
    count = gradient_piece.shape[0]
    chans = wt.shape[-1]
    kernel_taps = [
        gradient_padded[2 * dilation_step : 2 * dilation_step + count],
        gradient_piece,
        gradient_padded[0:count],
    ]
    h_pix = split_pixels(h, chans)
    gh = jnp.zeros(gradient_piece.shape, jnp.float32)
    tgrads = []
    for k in range(3):
        tap = split_pixels(kernel_taps[k], chans)
        gh = gh + jnp.einsum(
            "trwd,cd->trwc", tap, wt[k], preferred_element_type=jnp.float32
        ).reshape(gradient_piece.shape)
        tgrads.append(jnp.einsum("trwc,trwd->cd", h_pix, tap, preferred_element_type=jnp.float32))
    return (gh.astype(jnp.bfloat16), jnp.stack(tgrads))


def section_backward(x, gradient_piece, ws, wt):
    dilation_step = TIME_DILATION
    z = spatial_fwd(x, ws)
    sig = jax.nn.sigmoid(z)
    h = (z * sig).astype(jnp.bfloat16)
    deriv = sig * (1.0 + z * (1.0 - sig))
    tile_gradient, h_tile = (
        lax.all_to_all(gradient_piece, "tm", split_axis=2, concat_axis=0, tiled=True),
        lax.all_to_all(h, "tm", split_axis=2, concat_axis=0, tiled=True),
    )
    gradient_padded = jnp.pad(tile_gradient, ((dilation_step, dilation_step), (0, 0), (0, 0)))
    gh_tile, tgrads = temporal_back(h_tile, tile_gradient, gradient_padded, dilation_step, wt)
    gh = lax.all_to_all(gh_tile, "tm", split_axis=0, concat_axis=2, tiled=True)
    gz = (gh.astype(jnp.float32) * deriv).astype(jnp.bfloat16)
    back, sgrads = spatial_back(gz, x, ws)
    result = (gradient_piece.astype(jnp.float32) + back).astype(jnp.bfloat16)
    return (result, sgrads, tgrads)


def body(acts, cot, spatial_weight, temporal_weight):
    section_idx = lax.axis_index("section")
    number_sections = lax.axis_size("section")
    micro = acts.shape[1]
    local_acts = acts[0]
    ws = spatial_weight[0]
    wt = temporal_weight[0]
    received = jnp.zeros(cot.shape[1:], jnp.bfloat16)
    grads_in = jnp.zeros(local_acts.shape, jnp.bfloat16)
    acc_spatial = jnp.zeros(ws.shape, jnp.float32)
    acc_temporal = jnp.zeros(wt.shape, jnp.float32)
    total_turns = micro + number_sections - 1
    for turn in range(total_turns):
        which = jnp.int32(turn) - (number_sections - 1 - section_idx)
        valid = jnp.logical_and(which >= 0, which < micro)
        clipped = jnp.clip(which, 0, micro - 1)
        x_now = lax.dynamic_index_in_dim(local_acts, clipped, 0, keepdims=False)
        top_grad = lax.dynamic_index_in_dim(cot, clipped, 0, keepdims=False)
        incoming = jnp.where(section_idx == number_sections - 1, top_grad, received)
        result, sgrads, tgrads = section_backward(x_now, incoming, ws, wt)
        weight = valid.astype(jnp.float32)
        acc_spatial = acc_spatial + weight * sgrads
        acc_temporal = acc_temporal + weight * tgrads
        select = (jnp.arange(micro, dtype=jnp.int32) == which)[:, None, None, None]
        grads_in = jnp.where(select, result[None], grads_in)
        if turn + 1 < total_turns:
            received = from_behind(result, "section", -1)
    sum_spatial, sum_temporal = lax.psum((acc_spatial, acc_temporal), ("tm", "batch"))
    return (grads_in[None], sum_spatial[None], sum_temporal[None])


def solution(mesh):
    in_specs = (
        P("section", "batch", "tm", None, None),
        P("batch", "tm", None, None),
        P("section", None, None, None),
        P("section", None, None, None),
    )
    out_specs = (
        P("section", "batch", "tm", None, None),
        P("section", None, None, None),
        P("section", None, None, None),
    )
    return jax.shard_map(body, mesh=mesh, in_specs=in_specs, out_specs=out_specs, check_vma=False)
```

profile of v0, /device:TPU:24, one launch (start us, length us, event | category | flops | bytes accessed | tf_op | source)
XLA Modules:
  0.0 929.5 jit_solution(14927379624928204376)
XLA Ops:
  8.3 8.2 copy.623
  16.6 10.0 %reshape.1685 = bf16[4,2,15360]{2,1,0:T(2,128)(2,1)} reshape(bf16[10240,2,6]{2,1,0:T(2,128)(2,1)} %bitcast.1159) | data formatting | bytes 491520
  26.5 4.2 all-to-all-start
  126.4 13.6 %reshape.1686 = bf16[10240,2,6]{2,1,0:T(2,128)(2,1)} reshape(bf16[4,2,15360]{2,1,0:T(2,128)(2,1)} %all-to-all-done) | data formatting | bytes 491520
  140.0 10.6 %copy.624 = bf16[2,6,4,2560]{3,0,2,1:T(2,128)(2,1)S(1)} copy(bf16[2,6,4,2560]{1,0,3,2:T(2,128)(2,1)} %bitcast.1160) | data formatting | bytes 491520 | tf_op jit(solution)/shard_map/all_to_all | solution.py:95
  153.7 4.3 all-to-all-start.1
  159.1 4.6 all-to-all-done.1
  205.2 10.3 %copy.809 = bf16[2,6,10240]{1,0,2:T(2,128)(2,1)} copy(bf16[2,6,10240]{2,0,1:T(2,128)(2,1)} %get-tuple-element.11) | data formatting | bytes 491520 | tf_op jit(solution)/shard_map/convert_element_type | solution.py:92
  215.5 9.9 %reshape.1695 = bf16[4,2,15360]{2,1,0:T(2,128)(2,1)} reshape(bf16[10240,2,6]{2,1,0:T(2,128)(2,1)} %bitcast.1161) | data formatting | bytes 491520
  233.9 8.2 copy.651
  242.1 9.9 %reshape.1687 = bf16[4,2,15360]{2,1,0:T(2,128)(2,1)} reshape(bf16[10240,2,6]{2,1,0:T(2,128)(2,1)} %bitcast.1175) | data formatting | bytes 491520
  257.1 12.6 %reshape.1696 = bf16[10240,2,6]{2,1,0:T(2,128)(2,1)} reshape(bf16[4,2,15360]{2,1,0:T(2,128)(2,1)S(1)} %all-to-all-done.10) | data formatting | bytes 491520
  269.7 12.2 %copy.902 = bf16[2,6,4,2560]{3,2,0,1:T(4,128)(2,1)S(1)} copy(bf16[2,6,4,2560]{1,0,3,2:T(2,128)(2,1)} %bitcast.1162) | data formatting | bytes 491520 | tf_op jit(solution)/shard_map/all_to_all | solution.py:96
  283.3 12.6 %reshape.1688 = bf16[10240,2,6]{2,1,0:T(2,128)(2,1)} reshape(bf16[4,2,15360]{2,1,0:T(2,128)(2,1)S(1)} %all-to-all-done.2) | data formatting | bytes 491520
  296.0 10.2 %copy.652 = bf16[2,6,4,2560]{3,0,2,1:T(2,128)(2,1)S(1)} copy(bf16[2,6,4,2560]{1,0,3,2:T(2,128)(2,1)} %bitcast.1163) | data formatting | bytes 491520 | tf_op jit(solution)/shard_map/all_to_all | solution.py:95
  314.8 4.4 all-to-all-start.3
  366.4 10.3 %copy.812 = bf16[2,6,10240]{1,0,2:T(2,128)(2,1)} copy(bf16[2,6,10240]{2,0,1:T(2,128)(2,1)} %get-tuple-element.9) | data formatting | bytes 491520 | tf_op jit(solution)/shard_map/convert_element_type | solution.py:92
  376.7 9.9 %reshape.1697 = bf16[4,2,15360]{2,1,0:T(2,128)(2,1)} reshape(bf16[10240,2,6]{2,1,0:T(2,128)(2,1)} %bitcast.1164) | data formatting | bytes 491520
  395.5 8.1 copy.679
  403.7 9.9 %reshape.1689 = bf16[4,2,15360]{2,1,0:T(2,128)(2,1)} reshape(bf16[10240,2,6]{2,1,0:T(2,128)(2,1)} %bitcast.1176) | data formatting | bytes 491520
  418.4 12.6 %reshape.1698 = bf16[10240,2,6]{2,1,0:T(2,128)(2,1)} reshape(bf16[4,2,15360]{2,1,0:T(2,128)(2,1)S(1)} %all-to-all-done.11) | data formatting | bytes 491520
  431.1 12.2 %copy.903 = bf16[2,6,4,2560]{3,2,0,1:T(4,128)(2,1)S(1)} copy(bf16[2,6,4,2560]{1,0,3,2:T(2,128)(2,1)} %bitcast.1165) | data formatting | bytes 491520 | tf_op jit(solution)/shard_map/all_to_all | solution.py:96
  444.7 12.6 %reshape.1690 = bf16[10240,2,6]{2,1,0:T(2,128)(2,1)} reshape(bf16[4,2,15360]{2,1,0:T(2,128)(2,1)S(1)} %all-to-all-done.4) | data formatting | bytes 491520
  457.3 10.2 %copy.680 = bf16[2,6,4,2560]{3,0,2,1:T(2,128)(2,1)S(1)} copy(bf16[2,6,4,2560]{1,0,3,2:T(2,128)(2,1)} %bitcast.1166) | data formatting | bytes 491520 | tf_op jit(solution)/shard_map/all_to_all | solution.py:95
  476.2 4.4 all-to-all-start.5
  525.7 10.2 %copy.815 = bf16[2,6,10240]{1,0,2:T(2,128)(2,1)} copy(bf16[2,6,10240]{2,0,1:T(2,128)(2,1)} %get-tuple-element.7) | data formatting | bytes 491520 | tf_op jit(solution)/shard_map/convert_element_type | solution.py:92
  536.0 9.9 %reshape.1699 = bf16[4,2,15360]{2,1,0:T(2,128)(2,1)} reshape(bf16[10240,2,6]{2,1,0:T(2,128)(2,1)} %bitcast.1167) | data formatting | bytes 491520
  554.6 8.1 copy.707
  562.8 9.9 %reshape.1691 = bf16[4,2,15360]{2,1,0:T(2,128)(2,1)} reshape(bf16[10240,2,6]{2,1,0:T(2,128)(2,1)} %bitcast.1177) | data formatting | bytes 491520
  577.8 12.6 %reshape.1700 = bf16[10240,2,6]{2,1,0:T(2,128)(2,1)} reshape(bf16[4,2,15360]{2,1,0:T(2,128)(2,1)S(1)} %all-to-all-done.12) | data formatting | bytes 491520
  590.4 12.2 %copy.904 = bf16[2,6,4,2560]{3,2,0,1:T(4,128)(2,1)S(1)} copy(bf16[2,6,4,2560]{1,0,3,2:T(2,128)(2,1)} %bitcast.1168) | data formatting | bytes 491520 | tf_op jit(solution)/shard_map/all_to_all | solution.py:96
  604.0 12.6 %reshape.1692 = bf16[10240,2,6]{2,1,0:T(2,128)(2,1)} reshape(bf16[4,2,15360]{2,1,0:T(2,128)(2,1)S(1)} %all-to-all-done.6) | data formatting | bytes 491520
  616.6 10.2 %copy.708 = bf16[2,6,4,2560]{3,0,2,1:T(2,128)(2,1)S(1)} copy(bf16[2,6,4,2560]{1,0,3,2:T(2,128)(2,1)} %bitcast.1169) | data formatting | bytes 491520 | tf_op jit(solution)/shard_map/all_to_all | solution.py:95
  635.5 4.6 all-to-all-start.7
  687.6 10.2 %copy.818 = bf16[2,6,10240]{1,0,2:T(2,128)(2,1)} copy(bf16[2,6,10240]{2,0,1:T(2,128)(2,1)} %get-tuple-element.5) | data formatting | bytes 491520 | tf_op jit(solution)/shard_map/convert_element_type | solution.py:92
  697.8 9.9 %reshape.1701 = bf16[4,2,15360]{2,1,0:T(2,128)(2,1)} reshape(bf16[10240,2,6]{2,1,0:T(2,128)(2,1)} %bitcast.1170) | data formatting | bytes 491520
  712.9 8.1 copy.735
  721.1 9.9 %reshape.1693 = bf16[4,2,15360]{2,1,0:T(2,128)(2,1)} reshape(bf16[10240,2,6]{2,1,0:T(2,128)(2,1)} %bitcast.1178) | data formatting | bytes 491520
  735.9 12.6 %reshape.1702 = bf16[10240,2,6]{2,1,0:T(2,128)(2,1)} reshape(bf16[4,2,15360]{2,1,0:T(2,128)(2,1)S(1)} %all-to-all-done.13) | data formatting | bytes 491520
  748.5 12.2 %copy.905 = bf16[2,6,4,2560]{3,2,0,1:T(4,128)(2,1)S(1)} copy(bf16[2,6,4,2560]{1,0,3,2:T(2,128)(2,1)} %bitcast.1171) | data formatting | bytes 491520 | tf_op jit(solution)/shard_map/all_to_all | solution.py:96
  762.1 12.6 %reshape.1694 = bf16[10240,2,6]{2,1,0:T(2,128)(2,1)} reshape(bf16[4,2,15360]{2,1,0:T(2,128)(2,1)S(1)} %all-to-all-done.8) | data formatting | bytes 491520
  774.7 10.2 %copy.736 = bf16[2,6,4,2560]{3,0,2,1:T(2,128)(2,1)S(1)} copy(bf16[2,6,4,2560]{1,0,3,2:T(2,128)(2,1)} %bitcast.1172) | data formatting | bytes 491520 | tf_op jit(solution)/shard_map/all_to_all | solution.py:95
  788.7 4.3 all-to-all-start.9
  841.1 10.3 %copy.821 = bf16[2,6,10240]{1,0,2:T(2,128)(2,1)} copy(bf16[2,6,10240]{2,0,1:T(2,128)(2,1)} %get-tuple-element.3) | data formatting | bytes 491520 | tf_op jit(solution)/shard_map/convert_element_type | solution.py:92
  851.4 9.9 %reshape.1703 = bf16[4,2,15360]{2,1,0:T(2,128)(2,1)} reshape(bf16[10240,2,6]{2,1,0:T(2,128)(2,1)} %bitcast.1173) | data formatting | bytes 491520
  870.4 12.6 %reshape.1704 = bf16[10240,2,6]{2,1,0:T(2,128)(2,1)} reshape(bf16[4,2,15360]{2,1,0:T(2,128)(2,1)S(1)} %all-to-all-done.14) | data formatting | bytes 491520
  883.2 12.3 %copy.906 = bf16[2,6,4,2560]{3,2,0,1:T(4,128)(2,1)S(1)} copy(bf16[2,6,4,2560]{1,0,3,2:T(2,128)(2,1)} %bitcast.1174) | data formatting | bytes 491520 | tf_op jit(solution)/shard_map/all_to_all | solution.py:96
  897.0 23.7 %psum.15 = f32[1,3,64,64]{3,2,1,0:T(8,128)} all-reduce(f32[1,3,64,64]{3,2,1,0:T(8,128)S(1)} %fusion.170), channel_id=1, replica_groups=mesh['section'=4,'tm'=4,'batch'=2] {'tm','batch'}, use_global_device_ids=true, to_apply=%region_1.2 | all-reduce | flops 12288 | bytes 98304 | tf_op jit(solution)/shard_map/psum | solution.py:134
  (812 shorter events, 426.2 us)
Async XLA Ops:
  26.5 99.9 %all-to-all-start = ((bf16[4,2,15360]{2,1,0:T(2,128)(2,1)}), bf16[4,2,15360]{2,1,0:T(2,128)(2,1)}, u32[]{:S(2)}, u32[]{:S(2)}) async-start(bf16[4,2,15360]{2,1,0:T(2,128)(2,1)} %reshape.1685), calls=%async_computation | async-start | bytes 491520 | tf_op jit(solution)/shard_map/all_to_all | solution.py:95
  33.8 160.6 %copy-start.16 = (bf16[128,128,1,1]{1,0,2,3:T(8,128)(2,1)}, bf16[128,128,1,1]{1,0,2,3:T(8,128)(2,1)S(1)}, u32[]{:S(2)}) copy-start(bf16[128,128,1,1]{1,0,2,3:T(8,128)(2,1)S(1)} %reshape.1603) | copy-start | bytes 98308
  33.9 160.8 %copy-start.11 = (bf16[128,128,1,1]{1,0,2,3:T(8,128)(2,1)}, bf16[128,128,1,1]{1,0,2,3:T(8,128)(2,1)S(1)}, u32[]{:S(2)}) copy-start(bf16[128,128,1,1]{1,0,2,3:T(8,128)(2,1)S(1)} %reshape.1604) | copy-start | bytes 98308
  34.1 160.9 %copy-start.6 = (bf16[128,128,1,1]{1,0,2,3:T(8,128)(2,1)}, bf16[128,128,1,1]{1,0,2,3:T(8,128)(2,1)S(1)}, u32[]{:S(2)}) copy-start(bf16[128,128,1,1]{1,0,2,3:T(8,128)(2,1)S(1)} %reshape.1605) | copy-start | bytes 98308
  34.2 162.0 %copy-start.1 = (bf16[128,128,1,1]{1,0,2,3:T(8,128)(2,1)}, bf16[128,128,1,1]{1,0,2,3:T(8,128)(2,1)S(1)}, u32[]{:S(2)}) copy-start(bf16[128,128,1,1]{1,0,2,3:T(8,128)(2,1)S(1)} %reshape.1606) | copy-start | bytes 98308
  34.6 159.6 %copy-start.21 = (bf16[128,128,1,1]{1,0,2,3:T(8,128)(2,1)}, bf16[128,128,1,1]{1,0,2,3:T(8,128)(2,1)S(1)}, u32[]{:S(2)}) copy-start(bf16[128,128,1,1]{1,0,2,3:T(8,128)(2,1)S(1)} %reshape.1602) | copy-start | bytes 98308
  35.7 90.1 %copy-start.43 = (bf16[2,6,80,128]{3,2,0,1:T(8,128)(2,1)}, bf16[2,6,80,128]{3,2,0,1:T(8,128)(2,1)S(1)}, u32[]{:S(2)}) copy-start(bf16[2,6,80,128]{3,2,0,1:T(8,128)(2,1)S(1)} %reshape.1505) | copy-start | bytes 737284
  153.7 9.9 %all-to-all-start.1 = ((bf16[8,6,2560]{2,1,0:T(8,128)(2,1)}), bf16[8,6,2560]{2,1,0:T(8,128)(2,1)S(1)}, u32[]{:S(2)}, u32[]{:S(2)}) async-start(bf16[8,6,2560]{2,1,0:T(8,128)(2,1)} %reshape.1671), calls=%async_computation.1 | async-start | bytes 655360 | tf_op jit(solution)/shard_map/all_to_all | solution.py:100
  202.7 31.0 %collective-permute-start = (bf16[2,6,10240]{2,0,1:T(2,128)(2,1)S(1)}, bf16[2,6,10240]{2,0,1:T(2,128)(2,1)S(1)}, u32[]{:S(2)}, u32[]{:S(2)}) collective-permute-start(bf16[2,6,10240]{2,0,1:T(2,128)(2,1)S(1)} %add_convert_fusion.5), channel_id=1, source_target_pairs={{8,0},{16,8},{24,16},{9,1},{17,9},{25,17},{10,2},{18,10},{26,18},{... | collective-permute-start | bytes 737288 | tf_op jit(solution)/shard_map/ppermute | solution.py:12
  205.1 25.1 %copy-start.162 = (f32[128,128]{1,0:T(8,128)S(1)}, f32[128,128]{1,0:T(8,128)}, u32[]{:S(2)}) copy-start(f32[128,128]{1,0:T(8,128)} %convolution_bitcast_fusion.41) | copy-start | bytes 196612
  205.1 25.7 %copy-start.158 = (f32[128,128]{1,0:T(8,128)S(1)}, f32[128,128]{1,0:T(8,128)}, u32[]{:S(2)}) copy-start(f32[128,128]{1,0:T(8,128)} %convolution_bitcast_fusion.40) | copy-start | bytes 196612
  205.1 26.4 %copy-start.154 = (f32[128,128]{1,0:T(8,128)S(1)}, f32[128,128]{1,0:T(8,128)}, u32[]{:S(2)}) copy-start(f32[128,128]{1,0:T(8,128)} %convolution_bitcast_fusion.39) | copy-start | bytes 196612
  205.1 27.1 %copy-start.150 = (f32[128,128]{1,0:T(8,128)S(1)}, f32[128,128]{1,0:T(8,128)}, u32[]{:S(2)}) copy-start(f32[128,128]{1,0:T(8,128)} %convolution_bitcast_fusion.38) | copy-start | bytes 196612
  205.1 27.8 %copy-start.149 = (f32[128,128]{1,0:T(8,128)S(1)}, f32[128,128]{1,0:T(8,128)}, u32[]{:S(2)}) copy-start(f32[128,128]{1,0:T(8,128)} %convolution_bitcast_fusion.37) | copy-start | bytes 196612
  225.4 26.6 %all-to-all-start.10 = ((bf16[4,2,15360]{2,1,0:T(2,128)(2,1)}), bf16[4,2,15360]{2,1,0:T(2,128)(2,1)S(1)}, u32[]{:S(2)}, u32[]{:S(2)}) async-start(bf16[4,2,15360]{2,1,0:T(2,128)(2,1)} %reshape.1695), calls=%async_computation.10 | async-start | bytes 491520 | tf_op jit(solution)/shard_map/all_to_all | solution.py:96
  252.0 31.3 %all-to-all-start.2 = ((bf16[4,2,15360]{2,1,0:T(2,128)(2,1)}), bf16[4,2,15360]{2,1,0:T(2,128)(2,1)S(1)}, u32[]{:S(2)}, u32[]{:S(2)}) async-start(bf16[4,2,15360]{2,1,0:T(2,128)(2,1)} %reshape.1687), calls=%async_computation.2 | async-start | bytes 491520 | tf_op jit(solution)/shard_map/all_to_all | solution.py:95
  314.8 10.0 %all-to-all-start.3 = ((bf16[8,6,2560]{2,1,0:T(8,128)(2,1)}), bf16[8,6,2560]{2,1,0:T(8,128)(2,1)}, u32[]{:S(2)}, u32[]{:S(2)}) async-start(bf16[8,6,2560]{2,1,0:T(8,128)(2,1)} %reshape.1681), calls=%async_computation.3 | async-start | bytes 655360 | tf_op jit(solution)/shard_map/all_to_all | solution.py:100
  364.0 31.2 %collective-permute-start.1 = (bf16[2,6,10240]{2,0,1:T(2,128)(2,1)S(1)}, bf16[2,6,10240]{2,0,1:T(2,128)(2,1)S(1)}, u32[]{:S(2)}, u32[]{:S(2)}) collective-permute-start(bf16[2,6,10240]{2,0,1:T(2,128)(2,1)S(1)} %add_convert_fusion.4), channel_id=1, source_target_pairs={{8,0},{16,8},{24,16},{9,1},{17,9},{25,17},{10,2},{18,10},{26,18},{... | collective-permute-start | bytes 737288 | tf_op jit(solution)/shard_map/ppermute | solution.py:12
  366.4 25.4 %copy-start.167 = (f32[128,128]{1,0:T(8,128)S(1)}, f32[128,128]{1,0:T(8,128)}, u32[]{:S(2)}) copy-start(f32[128,128]{1,0:T(8,128)} %convolution_bitcast_fusion.32) | copy-start | bytes 196612
  366.4 26.1 %copy-start.163 = (f32[128,128]{1,0:T(8,128)S(1)}, f32[128,128]{1,0:T(8,128)}, u32[]{:S(2)}) copy-start(f32[128,128]{1,0:T(8,128)} %convolution_bitcast_fusion.31) | copy-start | bytes 196612
  366.4 26.8 %copy-start.159 = (f32[128,128]{1,0:T(8,128)S(1)}, f32[128,128]{1,0:T(8,128)}, u32[]{:S(2)}) copy-start(f32[128,128]{1,0:T(8,128)} %convolution_bitcast_fusion.30) | copy-start | bytes 196612
  366.4 27.4 %copy-start.155 = (f32[128,128]{1,0:T(8,128)S(1)}, f32[128,128]{1,0:T(8,128)}, u32[]{:S(2)}) copy-start(f32[128,128]{1,0:T(8,128)} %convolution_bitcast_fusion.29) | copy-start | bytes 196612
  366.4 28.1 %copy-start.151 = (f32[128,128]{1,0:T(8,128)S(1)}, f32[128,128]{1,0:T(8,128)}, u32[]{:S(2)}) copy-start(f32[128,128]{1,0:T(8,128)} %convolution_bitcast_fusion.28) | copy-start | bytes 196612
  386.6 26.9 %all-to-all-start.11 = ((bf16[4,2,15360]{2,1,0:T(2,128)(2,1)}), bf16[4,2,15360]{2,1,0:T(2,128)(2,1)S(1)}, u32[]{:S(2)}, u32[]{:S(2)}) async-start(bf16[4,2,15360]{2,1,0:T(2,128)(2,1)} %reshape.1697), calls=%async_computation.11 | async-start | bytes 491520 | tf_op jit(solution)/shard_map/all_to_all | solution.py:96
  413.6 31.1 %all-to-all-start.4 = ((bf16[4,2,15360]{2,1,0:T(2,128)(2,1)}), bf16[4,2,15360]{2,1,0:T(2,128)(2,1)S(1)}, u32[]{:S(2)}, u32[]{:S(2)}) async-start(bf16[4,2,15360]{2,1,0:T(2,128)(2,1)} %reshape.1689), calls=%async_computation.4 | async-start | bytes 491520 | tf_op jit(solution)/shard_map/all_to_all | solution.py:95
  476.2 10.0 %all-to-all-start.5 = ((bf16[8,6,2560]{2,1,0:T(8,128)(2,1)}), bf16[8,6,2560]{2,1,0:T(8,128)(2,1)}, u32[]{:S(2)}, u32[]{:S(2)}) async-start(bf16[8,6,2560]{2,1,0:T(8,128)(2,1)} %reshape.1682), calls=%async_computation.5 | async-start | bytes 655360 | tf_op jit(solution)/shard_map/all_to_all | solution.py:100
  523.5 30.9 %collective-permute-start.2 = (bf16[2,6,10240]{2,0,1:T(2,128)(2,1)S(1)}, bf16[2,6,10240]{2,0,1:T(2,128)(2,1)S(1)}, u32[]{:S(2)}, u32[]{:S(2)}) collective-permute-start(bf16[2,6,10240]{2,0,1:T(2,128)(2,1)S(1)} %add_convert_fusion.3), channel_id=1, source_target_pairs={{8,0},{16,8},{24,16},{9,1},{17,9},{25,17},{10,2},{18,10},{26,18},{... | collective-permute-start | bytes 737288 | tf_op jit(solution)/shard_map/ppermute | solution.py:12
  525.7 25.2 %copy-start.169 = (f32[128,128]{1,0:T(8,128)S(1)}, f32[128,128]{1,0:T(8,128)}, u32[]{:S(2)}) copy-start(f32[128,128]{1,0:T(8,128)} %convolution_bitcast_fusion.23) | copy-start | bytes 196612
  525.7 25.9 %copy-start.165 = (f32[128,128]{1,0:T(8,128)S(1)}, f32[128,128]{1,0:T(8,128)}, u32[]{:S(2)}) copy-start(f32[128,128]{1,0:T(8,128)} %convolution_bitcast_fusion.22) | copy-start | bytes 196612
  525.7 26.6 %copy-start.161 = (f32[128,128]{1,0:T(8,128)S(1)}, f32[128,128]{1,0:T(8,128)}, u32[]{:S(2)}) copy-start(f32[128,128]{1,0:T(8,128)} %convolution_bitcast_fusion.21) | copy-start | bytes 196612
  525.7 27.2 %copy-start.157 = (f32[128,128]{1,0:T(8,128)S(1)}, f32[128,128]{1,0:T(8,128)}, u32[]{:S(2)}) copy-start(f32[128,128]{1,0:T(8,128)} %convolution_bitcast_fusion.20) | copy-start | bytes 196612
  525.7 27.9 %copy-start.153 = (f32[128,128]{1,0:T(8,128)S(1)}, f32[128,128]{1,0:T(8,128)}, u32[]{:S(2)}) copy-start(f32[128,128]{1,0:T(8,128)} %convolution_bitcast_fusion.19) | copy-start | bytes 196612
  545.9 26.8 %all-to-all-start.12 = ((bf16[4,2,15360]{2,1,0:T(2,128)(2,1)}), bf16[4,2,15360]{2,1,0:T(2,128)(2,1)S(1)}, u32[]{:S(2)}, u32[]{:S(2)}) async-start(bf16[4,2,15360]{2,1,0:T(2,128)(2,1)} %reshape.1699), calls=%async_computation.12 | async-start | bytes 491520 | tf_op jit(solution)/shard_map/all_to_all | solution.py:96
  572.7 31.3 %all-to-all-start.6 = ((bf16[4,2,15360]{2,1,0:T(2,128)(2,1)}), bf16[4,2,15360]{2,1,0:T(2,128)(2,1)S(1)}, u32[]{:S(2)}, u32[]{:S(2)}) async-start(bf16[4,2,15360]{2,1,0:T(2,128)(2,1)} %reshape.1691), calls=%async_computation.6 | async-start | bytes 491520 | tf_op jit(solution)/shard_map/all_to_all | solution.py:95
  635.5 10.2 %all-to-all-start.7 = ((bf16[8,6,2560]{2,1,0:T(8,128)(2,1)}), bf16[8,6,2560]{2,1,0:T(8,128)(2,1)}, u32[]{:S(2)}, u32[]{:S(2)}) async-start(bf16[8,6,2560]{2,1,0:T(8,128)(2,1)} %reshape.1683), calls=%async_computation.7 | async-start | bytes 655360 | tf_op jit(solution)/shard_map/all_to_all | solution.py:100
  685.6 27.1 %collective-permute-start.3 = (bf16[2,6,10240]{2,0,1:T(2,128)(2,1)S(1)}, bf16[2,6,10240]{2,0,1:T(2,128)(2,1)S(1)}, u32[]{:S(2)}, u32[]{:S(2)}) collective-permute-start(bf16[2,6,10240]{2,0,1:T(2,128)(2,1)S(1)} %add_convert_fusion.2), channel_id=1, source_target_pairs={{8,0},{16,8},{24,16},{9,1},{17,9},{25,17},{10,2},{18,10},{26,18},{... | collective-permute-start | bytes 737288 | tf_op jit(solution)/shard_map/ppermute | solution.py:12
  687.5 24.6 %copy-start.171 = (f32[128,128]{1,0:T(8,128)S(1)}, f32[128,128]{1,0:T(8,128)}, u32[]{:S(2)}) copy-start(f32[128,128]{1,0:T(8,128)} %convolution_bitcast_fusion.15) | copy-start | bytes 196612
  687.5 24.7 %copy-start.168 = (f32[128,128]{1,0:T(8,128)S(1)}, f32[128,128]{1,0:T(8,128)}, u32[]{:S(2)}) copy-start(f32[128,128]{1,0:T(8,128)} %convolution_bitcast_fusion.14) | copy-start | bytes 196612
  687.5 24.7 %copy-start.164 = (f32[128,128]{1,0:T(8,128)S(1)}, f32[128,128]{1,0:T(8,128)}, u32[]{:S(2)}) copy-start(f32[128,128]{1,0:T(8,128)} %convolution_bitcast_fusion.13) | copy-start | bytes 196612
  687.6 24.8 %copy-start.160 = (f32[128,128]{1,0:T(8,128)S(1)}, f32[128,128]{1,0:T(8,128)}, u32[]{:S(2)}) copy-start(f32[128,128]{1,0:T(8,128)} %convolution_bitcast_fusion.12) | copy-start | bytes 196612
  687.6 24.9 %copy-start.156 = (f32[128,128]{1,0:T(8,128)S(1)}, f32[128,128]{1,0:T(8,128)}, u32[]{:S(2)}) copy-start(f32[128,128]{1,0:T(8,128)} %convolution_bitcast_fusion.11) | copy-start | bytes 196612
  687.6 25.0 %copy-start.152 = (f32[128,128]{1,0:T(8,128)S(1)}, f32[128,128]{1,0:T(8,128)}, u32[]{:S(2)}) copy-start(f32[128,128]{1,0:T(8,128)} %convolution_bitcast_fusion.10) | copy-start | bytes 196612
  707.7 23.3 %all-to-all-start.13 = ((bf16[4,2,15360]{2,1,0:T(2,128)(2,1)}), bf16[4,2,15360]{2,1,0:T(2,128)(2,1)S(1)}, u32[]{:S(2)}, u32[]{:S(2)}) async-start(bf16[4,2,15360]{2,1,0:T(2,128)(2,1)} %reshape.1701), calls=%async_computation.13 | async-start | bytes 491520 | tf_op jit(solution)/shard_map/all_to_all | solution.py:96
  731.0 31.1 %all-to-all-start.8 = ((bf16[4,2,15360]{2,1,0:T(2,128)(2,1)}), bf16[4,2,15360]{2,1,0:T(2,128)(2,1)S(1)}, u32[]{:S(2)}, u32[]{:S(2)}) async-start(bf16[4,2,15360]{2,1,0:T(2,128)(2,1)} %reshape.1693), calls=%async_computation.8 | async-start | bytes 491520 | tf_op jit(solution)/shard_map/all_to_all | solution.py:95
  735.9 24.8 %copy-start.122 = (f32[9,64,64]{2,1,0:T(8,128)}, f32[9,64,64]{2,1,0:T(8,128)S(1)}, u32[]{:S(2)}) copy-start(f32[9,64,64]{2,1,0:T(8,128)S(1)} %get-tuple-element.143) | copy-start | bytes 442372
  788.7 9.9 %all-to-all-start.9 = ((bf16[8,6,2560]{2,1,0:T(8,128)(2,1)}), bf16[8,6,2560]{2,1,0:T(8,128)(2,1)S(1)}, u32[]{:S(2)}, u32[]{:S(2)}) async-start(bf16[8,6,2560]{2,1,0:T(8,128)(2,1)} %reshape.1684), calls=%async_computation.9 | async-start | bytes 655360 | tf_op jit(solution)/shard_map/all_to_all | solution.py:100
  793.0 127.7 %all-reduce.17.cloned.1.call-start = ((), (), s32[]{:S(2)}) async-start(), calls=%async_computation.15 | async-start | bytes 589824 | tf_op jit(solution)/shard_map/psum | solution.py:134
  861.3 9.1 all-to-all-start.14
  (151 other events, 1933.2 us)
Sparse Core Ops, SparseCore 0:
  820.6 53.1 all-reduce.16
where the time goes:
time: 944 us; the launch traced here: 930 us
  local copies, waits for them, and re-layouts  609 us (65%)
  matrix products  137 us (15%)
  starting transfers between devices  70 us (7%)
  other arithmetic  49 us (5%)
  blocking collectives  23.7 us (3%)
  waiting for transfers between devices  23.2 us (2%)
  between operations  17.9 us (2%)
    unnamed x379, local copies, waits for them, and re-layouts  229 us
    reshape x105, local copies, waits for them, and re-layouts, split_pixels(): return a.reshape(a.shape[:-1] + (a.shape[-1] // chans, chans))  112 us
    all_to_all x10, local copies, waits for them, and re-layouts, section_backward(): lax.all_to_all(h, 'tm', split_axis=2, concat_axis=0, tiled=True)  61.8 us
    dot_general x45, matrix products, spatial_back(): jnp.einsum('nrpa,nrpb->ab', xpiece, gz_pairs, preferred_element_type=jnp....  54.5 us
    all_to_all x10, local copies, waits for them, and re-layouts, section_backward(): lax.all_to_all(gradient_piece, 'tm', split_axis=2, concat_axis=0, tiled=T...  52.1 us
    convert_element_type x5, local copies, waits for them, and re-layouts, section_backward(): h = (z * sig).astype(jnp.bfloat16)  51.3 us
    select_n x5, local copies, waits for them, and re-layouts, body(): incoming = jnp.where(section_idx == number_sections - 1, top_grad, received)  40.8 us
    dot_general x45, matrix products, spatial_fwd(): jnp.einsum('nrpa,ab->nrpb', piece, paired_kernel(ws[3 * i + j]), preferre...  28.6 us
  transfers between devices with their start and end apart: 20, of which 6 were waited for; matrix products, arithmetic and copies ran while one was open for 48% of the time, Pallas kernels for 0%

commit v1 on v0

--- a/solution.py
+++ b/solution.py
@@ -105,6 +105,12 @@
 
 
 def body(acts, cot, spatial_weight, temporal_weight):
+
+    def set_routes_all(own_rows, lane_axis, ax_name):
+        for idx in (lane_axis, ax_name):
+            own_rows = lax.psum(own_rows, idx)
+        return own_rows
+
     section_idx = lax.axis_index("section")
     number_sections = lax.axis_size("section")
     micro = acts.shape[1]
@@ -131,7 +137,7 @@
         grads_in = jnp.where(select, result[None], grads_in)
         if turn + 1 < total_turns:
             received = from_behind(result, "section", -1)
-    sum_spatial, sum_temporal = lax.psum((acc_spatial, acc_temporal), ("tm", "batch"))
+    sum_spatial, sum_temporal = set_routes_all((acc_spatial, acc_temporal), "tm", "batch")
     return (grads_in[None], sum_spatial[None], sum_temporal[None])
 
 

time: 944 us -> 941 us (level)
    psum x1 -> x2, blocking collectives: 23.7 us -> 20.6 us  [set_routes_all(): own_rows = lax.psum(own_rows, idx)]
  transfers between devices with their start and end apart: 20 -> 21, of which waited for: 6 -> 6; matrix products, arithmetic and copies ran while one was open for 48% -> 48% of each run, Pallas kernels for 0% -> 0%
where the time goes in v1:
time: 941 us; the launch traced here: 926 us
  local copies, waits for them, and re-layouts  609 us (65%)
  matrix products  137 us (15%)
  starting transfers between devices  70.1 us (7%)
  other arithmetic  48.9 us (5%)
  waiting for transfers between devices  22.6 us (2%)
  blocking collectives  20.6 us (2%)
  between operations  17.9 us (2%)
    unnamed x379, local copies, waits for them, and re-layouts  229 us
    reshape x105, local copies, waits for them, and re-layouts, split_pixels(): return a.reshape(a.shape[:-1] + (a.shape[-1] // chans, chans))  112 us
    all_to_all x10, local copies, waits for them, and re-layouts, section_backward(): lax.all_to_all(h, 'tm', split_axis=2, concat_axis=0, tiled=True)  61.8 us
    dot_general x45, matrix products, spatial_back(): jnp.einsum('nrpa,nrpb->ab', xpiece, gz_pairs, preferred_element_type=jnp....  54.6 us
    all_to_all x10, local copies, waits for them, and re-layouts, section_backward(): lax.all_to_all(gradient_piece, 'tm', split_axis=2, concat_axis=0, tiled=T...  52.1 us
    convert_element_type x5, local copies, waits for them, and re-layouts, section_backward(): h = (z * sig).astype(jnp.bfloat16)  51.3 us
    select_n x5, local copies, waits for them, and re-layouts, body(): incoming = jnp.where(section_idx == number_sections - 1, top_grad, received)  40.8 us
    dot_general x45, matrix products, spatial_fwd(): jnp.einsum('nrpa,ab->nrpb', piece, paired_kernel(ws[3 * i + j]), preferre...  28.7 us
  transfers between devices with their start and end apart: 21, of which 6 were waited for; matrix products, arithmetic and copies ran while one was open for 48% of the time, Pallas kernels for 0%

profile of v1, /device:TPU:24, one launch (start us, length us, event | category | flops | bytes accessed | tf_op | source)
XLA Modules:
  0.0 926.0 jit_solution(10682767116544210392)
XLA Ops:
  8.3 8.2 copy.623
  16.5 10.0 %reshape.1685 = bf16[4,2,15360]{2,1,0:T(2,128)(2,1)} reshape(bf16[10240,2,6]{2,1,0:T(2,128)(2,1)} %bitcast.1157) | data formatting | bytes 491520
  26.5 4.2 all-to-all-start
  126.2 13.6 %reshape.1686 = bf16[10240,2,6]{2,1,0:T(2,128)(2,1)} reshape(bf16[4,2,15360]{2,1,0:T(2,128)(2,1)} %all-to-all-done) | data formatting | bytes 491520
  139.9 10.6 %copy.624 = bf16[2,6,4,2560]{3,0,2,1:T(2,128)(2,1)S(1)} copy(bf16[2,6,4,2560]{1,0,3,2:T(2,128)(2,1)} %bitcast.1158) | data formatting | bytes 491520 | tf_op jit(solution)/shard_map/all_to_all | solution.py:95
  153.6 4.3 all-to-all-start.1
  158.9 4.5 all-to-all-done.1
  205.0 10.3 %copy.809 = bf16[2,6,10240]{1,0,2:T(2,128)(2,1)} copy(bf16[2,6,10240]{2,0,1:T(2,128)(2,1)} %get-tuple-element.11) | data formatting | bytes 491520 | tf_op jit(solution)/shard_map/convert_element_type | solution.py:92
  215.3 9.9 %reshape.1695 = bf16[4,2,15360]{2,1,0:T(2,128)(2,1)} reshape(bf16[10240,2,6]{2,1,0:T(2,128)(2,1)} %bitcast.1159) | data formatting | bytes 491520
  233.7 8.2 copy.651
  241.8 9.9 %reshape.1687 = bf16[4,2,15360]{2,1,0:T(2,128)(2,1)} reshape(bf16[10240,2,6]{2,1,0:T(2,128)(2,1)} %bitcast.1173) | data formatting | bytes 491520
  256.8 12.6 %reshape.1696 = bf16[10240,2,6]{2,1,0:T(2,128)(2,1)} reshape(bf16[4,2,15360]{2,1,0:T(2,128)(2,1)S(1)} %all-to-all-done.10) | data formatting | bytes 491520
  269.4 12.2 %copy.902 = bf16[2,6,4,2560]{3,2,0,1:T(4,128)(2,1)S(1)} copy(bf16[2,6,4,2560]{1,0,3,2:T(2,128)(2,1)} %bitcast.1160) | data formatting | bytes 491520 | tf_op jit(solution)/shard_map/all_to_all | solution.py:96
  283.0 12.6 %reshape.1688 = bf16[10240,2,6]{2,1,0:T(2,128)(2,1)} reshape(bf16[4,2,15360]{2,1,0:T(2,128)(2,1)S(1)} %all-to-all-done.2) | data formatting | bytes 491520
  295.6 10.2 %copy.652 = bf16[2,6,4,2560]{3,0,2,1:T(2,128)(2,1)S(1)} copy(bf16[2,6,4,2560]{1,0,3,2:T(2,128)(2,1)} %bitcast.1161) | data formatting | bytes 491520 | tf_op jit(solution)/shard_map/all_to_all | solution.py:95
  314.5 4.4 all-to-all-start.3
  366.2 10.3 %copy.812 = bf16[2,6,10240]{1,0,2:T(2,128)(2,1)} copy(bf16[2,6,10240]{2,0,1:T(2,128)(2,1)} %get-tuple-element.9) | data formatting | bytes 491520 | tf_op jit(solution)/shard_map/convert_element_type | solution.py:92
  376.5 9.9 %reshape.1697 = bf16[4,2,15360]{2,1,0:T(2,128)(2,1)} reshape(bf16[10240,2,6]{2,1,0:T(2,128)(2,1)} %bitcast.1162) | data formatting | bytes 491520
  395.3 8.1 copy.679
  403.5 9.9 %reshape.1689 = bf16[4,2,15360]{2,1,0:T(2,128)(2,1)} reshape(bf16[10240,2,6]{2,1,0:T(2,128)(2,1)} %bitcast.1174) | data formatting | bytes 491520
  418.3 12.6 %reshape.1698 = bf16[10240,2,6]{2,1,0:T(2,128)(2,1)} reshape(bf16[4,2,15360]{2,1,0:T(2,128)(2,1)S(1)} %all-to-all-done.11) | data formatting | bytes 491520
  430.9 12.2 %copy.903 = bf16[2,6,4,2560]{3,2,0,1:T(4,128)(2,1)S(1)} copy(bf16[2,6,4,2560]{1,0,3,2:T(2,128)(2,1)} %bitcast.1163) | data formatting | bytes 491520 | tf_op jit(solution)/shard_map/all_to_all | solution.py:96
  444.5 12.6 %reshape.1690 = bf16[10240,2,6]{2,1,0:T(2,128)(2,1)} reshape(bf16[4,2,15360]{2,1,0:T(2,128)(2,1)S(1)} %all-to-all-done.4) | data formatting | bytes 491520
  457.1 10.2 %copy.680 = bf16[2,6,4,2560]{3,0,2,1:T(2,128)(2,1)S(1)} copy(bf16[2,6,4,2560]{1,0,3,2:T(2,128)(2,1)} %bitcast.1164) | data formatting | bytes 491520 | tf_op jit(solution)/shard_map/all_to_all | solution.py:95
  476.0 4.4 all-to-all-start.5
  525.7 10.3 %copy.815 = bf16[2,6,10240]{1,0,2:T(2,128)(2,1)} copy(bf16[2,6,10240]{2,0,1:T(2,128)(2,1)} %get-tuple-element.7) | data formatting | bytes 491520 | tf_op jit(solution)/shard_map/convert_element_type | solution.py:92
  536.0 9.9 %reshape.1699 = bf16[4,2,15360]{2,1,0:T(2,128)(2,1)} reshape(bf16[10240,2,6]{2,1,0:T(2,128)(2,1)} %bitcast.1165) | data formatting | bytes 491520
  554.7 8.2 copy.707
  562.9 9.9 %reshape.1691 = bf16[4,2,15360]{2,1,0:T(2,128)(2,1)} reshape(bf16[10240,2,6]{2,1,0:T(2,128)(2,1)} %bitcast.1175) | data formatting | bytes 491520
  577.8 12.6 %reshape.1700 = bf16[10240,2,6]{2,1,0:T(2,128)(2,1)} reshape(bf16[4,2,15360]{2,1,0:T(2,128)(2,1)S(1)} %all-to-all-done.12) | data formatting | bytes 491520
  590.5 12.2 %copy.904 = bf16[2,6,4,2560]{3,2,0,1:T(4,128)(2,1)S(1)} copy(bf16[2,6,4,2560]{1,0,3,2:T(2,128)(2,1)} %bitcast.1166) | data formatting | bytes 491520 | tf_op jit(solution)/shard_map/all_to_all | solution.py:96
  604.0 12.6 %reshape.1692 = bf16[10240,2,6]{2,1,0:T(2,128)(2,1)} reshape(bf16[4,2,15360]{2,1,0:T(2,128)(2,1)S(1)} %all-to-all-done.6) | data formatting | bytes 491520
  616.7 10.2 %copy.708 = bf16[2,6,4,2560]{3,0,2,1:T(2,128)(2,1)S(1)} copy(bf16[2,6,4,2560]{1,0,3,2:T(2,128)(2,1)} %bitcast.1167) | data formatting | bytes 491520 | tf_op jit(solution)/shard_map/all_to_all | solution.py:95
  635.5 4.6 all-to-all-start.7
  687.7 10.2 %copy.818 = bf16[2,6,10240]{1,0,2:T(2,128)(2,1)} copy(bf16[2,6,10240]{2,0,1:T(2,128)(2,1)} %get-tuple-element.5) | data formatting | bytes 491520 | tf_op jit(solution)/shard_map/convert_element_type | solution.py:92
  697.9 9.9 %reshape.1701 = bf16[4,2,15360]{2,1,0:T(2,128)(2,1)} reshape(bf16[10240,2,6]{2,1,0:T(2,128)(2,1)} %bitcast.1168) | data formatting | bytes 491520
  713.0 8.1 copy.735
  721.1 9.9 %reshape.1693 = bf16[4,2,15360]{2,1,0:T(2,128)(2,1)} reshape(bf16[10240,2,6]{2,1,0:T(2,128)(2,1)} %bitcast.1176) | data formatting | bytes 491520
  735.9 12.6 %reshape.1702 = bf16[10240,2,6]{2,1,0:T(2,128)(2,1)} reshape(bf16[4,2,15360]{2,1,0:T(2,128)(2,1)S(1)} %all-to-all-done.13) | data formatting | bytes 491520
  748.5 12.2 %copy.905 = bf16[2,6,4,2560]{3,2,0,1:T(4,128)(2,1)S(1)} copy(bf16[2,6,4,2560]{1,0,3,2:T(2,128)(2,1)} %bitcast.1169) | data formatting | bytes 491520 | tf_op jit(solution)/shard_map/all_to_all | solution.py:96
  762.1 12.6 %reshape.1694 = bf16[10240,2,6]{2,1,0:T(2,128)(2,1)} reshape(bf16[4,2,15360]{2,1,0:T(2,128)(2,1)S(1)} %all-to-all-done.8) | data formatting | bytes 491520
  774.7 10.2 %copy.736 = bf16[2,6,4,2560]{3,0,2,1:T(2,128)(2,1)S(1)} copy(bf16[2,6,4,2560]{1,0,3,2:T(2,128)(2,1)} %bitcast.1170) | data formatting | bytes 491520 | tf_op jit(solution)/shard_map/all_to_all | solution.py:95
  788.7 4.3 all-to-all-start.9
  841.1 10.3 %copy.821 = bf16[2,6,10240]{1,0,2:T(2,128)(2,1)} copy(bf16[2,6,10240]{2,0,1:T(2,128)(2,1)} %get-tuple-element.3) | data formatting | bytes 491520 | tf_op jit(solution)/shard_map/convert_element_type | solution.py:92
  851.4 9.9 %reshape.1703 = bf16[4,2,15360]{2,1,0:T(2,128)(2,1)} reshape(bf16[10240,2,6]{2,1,0:T(2,128)(2,1)} %bitcast.1171) | data formatting | bytes 491520
  870.0 12.6 %reshape.1704 = bf16[10240,2,6]{2,1,0:T(2,128)(2,1)} reshape(bf16[4,2,15360]{2,1,0:T(2,128)(2,1)S(1)} %all-to-all-done.14) | data formatting | bytes 491520
  882.7 12.3 %copy.906 = bf16[2,6,4,2560]{3,2,0,1:T(4,128)(2,1)S(1)} copy(bf16[2,6,4,2560]{1,0,3,2:T(2,128)(2,1)} %bitcast.1172) | data formatting | bytes 491520 | tf_op jit(solution)/shard_map/all_to_all | solution.py:96
  896.6 16.4 %psum.30 = f32[3,64,64]{2,1,0:T(8,128)S(1)} all-reduce(f32[3,64,64]{2,1,0:T(8,128)S(1)} %fusion.169), channel_id=1, replica_groups=mesh['section'=4,'tm'=4,'batch'=2] {'tm'}, use_global_device_ids=true, to_apply=%region_2.3 | all-reduce | flops 12288 | bytes 98304 | tf_op jit(solution)/shard_map/psum | solution.py:111
  (816 shorter events, 430.2 us)
Async XLA Ops:
  26.5 99.8 %all-to-all-start = ((bf16[4,2,15360]{2,1,0:T(2,128)(2,1)}), bf16[4,2,15360]{2,1,0:T(2,128)(2,1)}, u32[]{:S(2)}, u32[]{:S(2)}) async-start(bf16[4,2,15360]{2,1,0:T(2,128)(2,1)} %reshape.1685), calls=%async_computation | async-start | bytes 491520 | tf_op jit(solution)/shard_map/all_to_all | solution.py:95
  33.7 160.6 %copy-start.16 = (bf16[128,128,1,1]{1,0,2,3:T(8,128)(2,1)}, bf16[128,128,1,1]{1,0,2,3:T(8,128)(2,1)S(1)}, u32[]{:S(2)}) copy-start(bf16[128,128,1,1]{1,0,2,3:T(8,128)(2,1)S(1)} %reshape.1603) | copy-start | bytes 98308
  33.8 160.7 %copy-start.11 = (bf16[128,128,1,1]{1,0,2,3:T(8,128)(2,1)}, bf16[128,128,1,1]{1,0,2,3:T(8,128)(2,1)S(1)}, u32[]{:S(2)}) copy-start(bf16[128,128,1,1]{1,0,2,3:T(8,128)(2,1)S(1)} %reshape.1604) | copy-start | bytes 98308
  33.9 160.8 %copy-start.6 = (bf16[128,128,1,1]{1,0,2,3:T(8,128)(2,1)}, bf16[128,128,1,1]{1,0,2,3:T(8,128)(2,1)S(1)}, u32[]{:S(2)}) copy-start(bf16[128,128,1,1]{1,0,2,3:T(8,128)(2,1)S(1)} %reshape.1605) | copy-start | bytes 98308
  34.1 162.0 %copy-start.1 = (bf16[128,128,1,1]{1,0,2,3:T(8,128)(2,1)}, bf16[128,128,1,1]{1,0,2,3:T(8,128)(2,1)S(1)}, u32[]{:S(2)}) copy-start(bf16[128,128,1,1]{1,0,2,3:T(8,128)(2,1)S(1)} %reshape.1606) | copy-start | bytes 98308
  34.5 159.6 %copy-start.21 = (bf16[128,128,1,1]{1,0,2,3:T(8,128)(2,1)}, bf16[128,128,1,1]{1,0,2,3:T(8,128)(2,1)S(1)}, u32[]{:S(2)}) copy-start(bf16[128,128,1,1]{1,0,2,3:T(8,128)(2,1)S(1)} %reshape.1602) | copy-start | bytes 98308
  35.6 90.0 %copy-start.43 = (bf16[2,6,80,128]{3,2,0,1:T(8,128)(2,1)}, bf16[2,6,80,128]{3,2,0,1:T(8,128)(2,1)S(1)}, u32[]{:S(2)}) copy-start(bf16[2,6,80,128]{3,2,0,1:T(8,128)(2,1)S(1)} %reshape.1505) | copy-start | bytes 737284
  153.6 9.9 %all-to-all-start.1 = ((bf16[8,6,2560]{2,1,0:T(8,128)(2,1)}), bf16[8,6,2560]{2,1,0:T(8,128)(2,1)S(1)}, u32[]{:S(2)}, u32[]{:S(2)}) async-start(bf16[8,6,2560]{2,1,0:T(8,128)(2,1)} %reshape.1671), calls=%async_computation.1 | async-start | bytes 655360 | tf_op jit(solution)/shard_map/all_to_all | solution.py:100
  202.5 30.9 %collective-permute-start = (bf16[2,6,10240]{2,0,1:T(2,128)(2,1)S(1)}, bf16[2,6,10240]{2,0,1:T(2,128)(2,1)S(1)}, u32[]{:S(2)}, u32[]{:S(2)}) collective-permute-start(bf16[2,6,10240]{2,0,1:T(2,128)(2,1)S(1)} %add_convert_fusion.5), channel_id=1, source_target_pairs={{8,0},{16,8},{24,16},{9,1},{17,9},{25,17},{10,2},{18,10},{26,18},{... | collective-permute-start | bytes 737288 | tf_op jit(solution)/shard_map/ppermute | solution.py:12
  204.9 25.0 %copy-start.162 = (f32[128,128]{1,0:T(8,128)S(1)}, f32[128,128]{1,0:T(8,128)}, u32[]{:S(2)}) copy-start(f32[128,128]{1,0:T(8,128)} %convolution_bitcast_fusion.41) | copy-start | bytes 196612
  204.9 25.7 %copy-start.158 = (f32[128,128]{1,0:T(8,128)S(1)}, f32[128,128]{1,0:T(8,128)}, u32[]{:S(2)}) copy-start(f32[128,128]{1,0:T(8,128)} %convolution_bitcast_fusion.40) | copy-start | bytes 196612
  205.0 26.4 %copy-start.154 = (f32[128,128]{1,0:T(8,128)S(1)}, f32[128,128]{1,0:T(8,128)}, u32[]{:S(2)}) copy-start(f32[128,128]{1,0:T(8,128)} %convolution_bitcast_fusion.39) | copy-start | bytes 196612
  205.0 27.0 %copy-start.150 = (f32[128,128]{1,0:T(8,128)S(1)}, f32[128,128]{1,0:T(8,128)}, u32[]{:S(2)}) copy-start(f32[128,128]{1,0:T(8,128)} %convolution_bitcast_fusion.38) | copy-start | bytes 196612
  205.0 27.7 %copy-start.149 = (f32[128,128]{1,0:T(8,128)S(1)}, f32[128,128]{1,0:T(8,128)}, u32[]{:S(2)}) copy-start(f32[128,128]{1,0:T(8,128)} %convolution_bitcast_fusion.37) | copy-start | bytes 196612
  225.2 26.6 %all-to-all-start.10 = ((bf16[4,2,15360]{2,1,0:T(2,128)(2,1)}), bf16[4,2,15360]{2,1,0:T(2,128)(2,1)S(1)}, u32[]{:S(2)}, u32[]{:S(2)}) async-start(bf16[4,2,15360]{2,1,0:T(2,128)(2,1)} %reshape.1695), calls=%async_computation.10 | async-start | bytes 491520 | tf_op jit(solution)/shard_map/all_to_all | solution.py:96
  251.7 31.3 %all-to-all-start.2 = ((bf16[4,2,15360]{2,1,0:T(2,128)(2,1)}), bf16[4,2,15360]{2,1,0:T(2,128)(2,1)S(1)}, u32[]{:S(2)}, u32[]{:S(2)}) async-start(bf16[4,2,15360]{2,1,0:T(2,128)(2,1)} %reshape.1687), calls=%async_computation.2 | async-start | bytes 491520 | tf_op jit(solution)/shard_map/all_to_all | solution.py:95
  314.5 10.0 %all-to-all-start.3 = ((bf16[8,6,2560]{2,1,0:T(8,128)(2,1)}), bf16[8,6,2560]{2,1,0:T(8,128)(2,1)}, u32[]{:S(2)}, u32[]{:S(2)}) async-start(bf16[8,6,2560]{2,1,0:T(8,128)(2,1)} %reshape.1681), calls=%async_computation.3 | async-start | bytes 655360 | tf_op jit(solution)/shard_map/all_to_all | solution.py:100
  363.7 31.3 %collective-permute-start.1 = (bf16[2,6,10240]{2,0,1:T(2,128)(2,1)S(1)}, bf16[2,6,10240]{2,0,1:T(2,128)(2,1)S(1)}, u32[]{:S(2)}, u32[]{:S(2)}) collective-permute-start(bf16[2,6,10240]{2,0,1:T(2,128)(2,1)S(1)} %add_convert_fusion.4), channel_id=1, source_target_pairs={{8,0},{16,8},{24,16},{9,1},{17,9},{25,17},{10,2},{18,10},{26,18},{... | collective-permute-start | bytes 737288 | tf_op jit(solution)/shard_map/ppermute | solution.py:12
  366.2 25.4 %copy-start.167 = (f32[128,128]{1,0:T(8,128)S(1)}, f32[128,128]{1,0:T(8,128)}, u32[]{:S(2)}) copy-start(f32[128,128]{1,0:T(8,128)} %convolution_bitcast_fusion.32) | copy-start | bytes 196612
  366.2 26.1 %copy-start.163 = (f32[128,128]{1,0:T(8,128)S(1)}, f32[128,128]{1,0:T(8,128)}, u32[]{:S(2)}) copy-start(f32[128,128]{1,0:T(8,128)} %convolution_bitcast_fusion.31) | copy-start | bytes 196612
  366.2 26.8 %copy-start.159 = (f32[128,128]{1,0:T(8,128)S(1)}, f32[128,128]{1,0:T(8,128)}, u32[]{:S(2)}) copy-start(f32[128,128]{1,0:T(8,128)} %convolution_bitcast_fusion.30) | copy-start | bytes 196612
  366.2 27.5 %copy-start.155 = (f32[128,128]{1,0:T(8,128)S(1)}, f32[128,128]{1,0:T(8,128)}, u32[]{:S(2)}) copy-start(f32[128,128]{1,0:T(8,128)} %convolution_bitcast_fusion.29) | copy-start | bytes 196612
  366.2 28.2 %copy-start.151 = (f32[128,128]{1,0:T(8,128)S(1)}, f32[128,128]{1,0:T(8,128)}, u32[]{:S(2)}) copy-start(f32[128,128]{1,0:T(8,128)} %convolution_bitcast_fusion.28) | copy-start | bytes 196612
  386.4 27.0 %all-to-all-start.11 = ((bf16[4,2,15360]{2,1,0:T(2,128)(2,1)}), bf16[4,2,15360]{2,1,0:T(2,128)(2,1)S(1)}, u32[]{:S(2)}, u32[]{:S(2)}) async-start(bf16[4,2,15360]{2,1,0:T(2,128)(2,1)} %reshape.1697), calls=%async_computation.11 | async-start | bytes 491520 | tf_op jit(solution)/shard_map/all_to_all | solution.py:96
  413.4 31.1 %all-to-all-start.4 = ((bf16[4,2,15360]{2,1,0:T(2,128)(2,1)}), bf16[4,2,15360]{2,1,0:T(2,128)(2,1)S(1)}, u32[]{:S(2)}, u32[]{:S(2)}) async-start(bf16[4,2,15360]{2,1,0:T(2,128)(2,1)} %reshape.1689), calls=%async_computation.4 | async-start | bytes 491520 | tf_op jit(solution)/shard_map/all_to_all | solution.py:95
  476.0 10.0 %all-to-all-start.5 = ((bf16[8,6,2560]{2,1,0:T(8,128)(2,1)}), bf16[8,6,2560]{2,1,0:T(8,128)(2,1)}, u32[]{:S(2)}, u32[]{:S(2)}) async-start(bf16[8,6,2560]{2,1,0:T(8,128)(2,1)} %reshape.1682), calls=%async_computation.5 | async-start | bytes 655360 | tf_op jit(solution)/shard_map/all_to_all | solution.py:100
  523.5 30.9 %collective-permute-start.2 = (bf16[2,6,10240]{2,0,1:T(2,128)(2,1)S(1)}, bf16[2,6,10240]{2,0,1:T(2,128)(2,1)S(1)}, u32[]{:S(2)}, u32[]{:S(2)}) collective-permute-start(bf16[2,6,10240]{2,0,1:T(2,128)(2,1)S(1)} %add_convert_fusion.3), channel_id=1, source_target_pairs={{8,0},{16,8},{24,16},{9,1},{17,9},{25,17},{10,2},{18,10},{26,18},{... | collective-permute-start | bytes 737288 | tf_op jit(solution)/shard_map/ppermute | solution.py:12
  525.7 25.2 %copy-start.169 = (f32[128,128]{1,0:T(8,128)S(1)}, f32[128,128]{1,0:T(8,128)}, u32[]{:S(2)}) copy-start(f32[128,128]{1,0:T(8,128)} %convolution_bitcast_fusion.23) | copy-start | bytes 196612
  525.7 25.9 %copy-start.165 = (f32[128,128]{1,0:T(8,128)S(1)}, f32[128,128]{1,0:T(8,128)}, u32[]{:S(2)}) copy-start(f32[128,128]{1,0:T(8,128)} %convolution_bitcast_fusion.22) | copy-start | bytes 196612
  525.7 26.6 %copy-start.161 = (f32[128,128]{1,0:T(8,128)S(1)}, f32[128,128]{1,0:T(8,128)}, u32[]{:S(2)}) copy-start(f32[128,128]{1,0:T(8,128)} %convolution_bitcast_fusion.21) | copy-start | bytes 196612
  525.7 27.3 %copy-start.157 = (f32[128,128]{1,0:T(8,128)S(1)}, f32[128,128]{1,0:T(8,128)}, u32[]{:S(2)}) copy-start(f32[128,128]{1,0:T(8,128)} %convolution_bitcast_fusion.20) | copy-start | bytes 196612
  525.7 28.0 %copy-start.153 = (f32[128,128]{1,0:T(8,128)S(1)}, f32[128,128]{1,0:T(8,128)}, u32[]{:S(2)}) copy-start(f32[128,128]{1,0:T(8,128)} %convolution_bitcast_fusion.19) | copy-start | bytes 196612
  545.9 26.9 %all-to-all-start.12 = ((bf16[4,2,15360]{2,1,0:T(2,128)(2,1)}), bf16[4,2,15360]{2,1,0:T(2,128)(2,1)S(1)}, u32[]{:S(2)}, u32[]{:S(2)}) async-start(bf16[4,2,15360]{2,1,0:T(2,128)(2,1)} %reshape.1699), calls=%async_computation.12 | async-start | bytes 491520 | tf_op jit(solution)/shard_map/all_to_all | solution.py:96
  572.8 31.3 %all-to-all-start.6 = ((bf16[4,2,15360]{2,1,0:T(2,128)(2,1)}), bf16[4,2,15360]{2,1,0:T(2,128)(2,1)S(1)}, u32[]{:S(2)}, u32[]{:S(2)}) async-start(bf16[4,2,15360]{2,1,0:T(2,128)(2,1)} %reshape.1691), calls=%async_computation.6 | async-start | bytes 491520 | tf_op jit(solution)/shard_map/all_to_all | solution.py:95
  635.5 10.2 %all-to-all-start.7 = ((bf16[8,6,2560]{2,1,0:T(8,128)(2,1)}), bf16[8,6,2560]{2,1,0:T(8,128)(2,1)}, u32[]{:S(2)}, u32[]{:S(2)}) async-start(bf16[8,6,2560]{2,1,0:T(8,128)(2,1)} %reshape.1683), calls=%async_computation.7 | async-start | bytes 655360 | tf_op jit(solution)/shard_map/all_to_all | solution.py:100
  685.7 27.0 %collective-permute-start.3 = (bf16[2,6,10240]{2,0,1:T(2,128)(2,1)S(1)}, bf16[2,6,10240]{2,0,1:T(2,128)(2,1)S(1)}, u32[]{:S(2)}, u32[]{:S(2)}) collective-permute-start(bf16[2,6,10240]{2,0,1:T(2,128)(2,1)S(1)} %add_convert_fusion.2), channel_id=1, source_target_pairs={{8,0},{16,8},{24,16},{9,1},{17,9},{25,17},{10,2},{18,10},{26,18},{... | collective-permute-start | bytes 737288 | tf_op jit(solution)/shard_map/ppermute | solution.py:12
  687.6 24.6 %copy-start.168 = (f32[128,128]{1,0:T(8,128)S(1)}, f32[128,128]{1,0:T(8,128)}, u32[]{:S(2)}) copy-start(f32[128,128]{1,0:T(8,128)} %convolution_bitcast_fusion.14) | copy-start | bytes 196612
  687.7 24.7 %copy-start.164 = (f32[128,128]{1,0:T(8,128)S(1)}, f32[128,128]{1,0:T(8,128)}, u32[]{:S(2)}) copy-start(f32[128,128]{1,0:T(8,128)} %convolution_bitcast_fusion.13) | copy-start | bytes 196612
  687.7 24.8 %copy-start.160 = (f32[128,128]{1,0:T(8,128)S(1)}, f32[128,128]{1,0:T(8,128)}, u32[]{:S(2)}) copy-start(f32[128,128]{1,0:T(8,128)} %convolution_bitcast_fusion.12) | copy-start | bytes 196612
  687.7 24.9 %copy-start.156 = (f32[128,128]{1,0:T(8,128)S(1)}, f32[128,128]{1,0:T(8,128)}, u32[]{:S(2)}) copy-start(f32[128,128]{1,0:T(8,128)} %convolution_bitcast_fusion.11) | copy-start | bytes 196612
  687.7 24.9 %copy-start.152 = (f32[128,128]{1,0:T(8,128)S(1)}, f32[128,128]{1,0:T(8,128)}, u32[]{:S(2)}) copy-start(f32[128,128]{1,0:T(8,128)} %convolution_bitcast_fusion.10) | copy-start | bytes 196612
  707.8 23.2 %all-to-all-start.13 = ((bf16[4,2,15360]{2,1,0:T(2,128)(2,1)}), bf16[4,2,15360]{2,1,0:T(2,128)(2,1)S(1)}, u32[]{:S(2)}, u32[]{:S(2)}) async-start(bf16[4,2,15360]{2,1,0:T(2,128)(2,1)} %reshape.1701), calls=%async_computation.13 | async-start | bytes 491520 | tf_op jit(solution)/shard_map/all_to_all | solution.py:96
  731.0 31.1 %all-to-all-start.8 = ((bf16[4,2,15360]{2,1,0:T(2,128)(2,1)}), bf16[4,2,15360]{2,1,0:T(2,128)(2,1)S(1)}, u32[]{:S(2)}, u32[]{:S(2)}) async-start(bf16[4,2,15360]{2,1,0:T(2,128)(2,1)} %reshape.1693), calls=%async_computation.8 | async-start | bytes 491520 | tf_op jit(solution)/shard_map/all_to_all | solution.py:95
  735.9 24.8 %copy-start.122 = (f32[9,64,64]{2,1,0:T(8,128)}, f32[9,64,64]{2,1,0:T(8,128)S(1)}, u32[]{:S(2)}) copy-start(f32[9,64,64]{2,1,0:T(8,128)S(1)} %get-tuple-element.143) | copy-start | bytes 442372
  788.7 9.9 %all-to-all-start.9 = ((bf16[8,6,2560]{2,1,0:T(8,128)(2,1)}), bf16[8,6,2560]{2,1,0:T(8,128)(2,1)S(1)}, u32[]{:S(2)}, u32[]{:S(2)}) async-start(bf16[8,6,2560]{2,1,0:T(8,128)(2,1)} %reshape.1684), calls=%async_computation.9 | async-start | bytes 655360 | tf_op jit(solution)/shard_map/all_to_all | solution.py:100
  793.0 73.8 %all-reduce.18.cloned.1.call-start = ((), (), s32[]{:S(2)}) async-start(), calls=%async_computation.15 | async-start | bytes 589824 | tf_op jit(solution)/shard_map/psum | solution.py:111
  861.3 8.7 all-to-all-start.14
  864.7 52.5 %all-reduce.20.cloned.1.call-start = ((), (), s32[]{:S(2)}) async-start(), calls=%async_computation.16 | async-start | bytes 589824 | tf_op jit(solution)/shard_map/psum | solution.py:111
  (152 other events, 1958.6 us)
Sparse Core Ops, SparseCore 0:
  820.6 43.2 all-reduce.17
  868.0 19.9 all-reduce.19
